TPU v7x, 128 devices: a whole 4x4x4 slice. The times are simulated.
128 devices in a mesh: tile: 64 (over x, y_hi, z, core), sub: 2 (over y_lo).
Axes of the slice: x: 4, y: 4 (y_hi: 2, y_lo: 2; y = y_hi * 2 + y_lo), z: 4, core: 2. Of those that a mesh axis runs over, the one named last changes fastest.
Arguments:
- pulses: bfloat16 [2, 64, 2, 64, 8192], P('sub', 'tile'), may hold values from -6 to 6
- kernel: bfloat16 [262144, 1024], P('tile'), may hold values from -0.1875 to 0.1875
- band_start: int32 [64, 1024], P('tile'), may hold values from 0 to 2048
- band_width: int32 [64, 1024], P('tile'), may hold values from 1 to 2048
- offset: int32 [64], P('tile'), may hold values from 0 to 4096
- owner: int32 [8], replicated, may hold values from 0 to 63, as said below
- angle: float32 [2, 8, 64, 65536], P('sub', None, None, 'tile'), may hold values from -3.140625 to 3.140625
- dest: int32 [4096, 1], P('tile'), may hold values from 0 to 63; in each aligned block of 64 rows (0 to 63, 64 to 127, ...) at most 2 rows name the same one
Outputs:
- merged: float32 [2, 1024, 1024], P(None, 'tile')
Inputs may be any that keep to these rules, and one draw needn't show every extreme that they name: `owner`: 8 different tile indices, among them the first and the last tile. `dest`: among the 64 strips of one tile, no parent tile is named more than 2 times.
All inputs are finite; a program needn't handle non-finite values.
Results may differ from a plain program's by a relative error of at most 0.0037.
Values may be sent and summed in bfloat16 or wider, within the bound.
No kernel may reach another device: no remote copies, remote signals or barrier semaphores. Data moves between devices by JAX's collectives and lax.ppermute only.
A program may use at most 192 MiB of HBM per device.

v0:
```python
import math

import jax
import jax.numpy as jnp
from jax import lax
from jax.sharding import PartitionSpec as P

STRIP = 16
CAP = 2


def broadcast(block, axis, owner):
    block = jnp.where(lax.axis_index(axis) == owner, block, jnp.zeros_like(block))
    return lax.psum(block, axis)


def phase_matrix(angle_tile, scale):
    cosine = (jnp.cos(angle_tile) * scale).T
    sine_part = (jnp.sin(angle_tile) * scale).T
    top_rows = jnp.concatenate([cosine, -sine_part], 1)
    low_rows = jnp.concatenate([sine_part, cosine], 1)
    return jnp.concatenate([top_rows, low_rows], 0).astype(jnp.bfloat16)


def pack_strips(subimage, dest):
    tile_count = dest.shape[0]
    strips = subimage.reshape(2, tile_count, STRIP, subimage.shape[1])
    targets = dest[:, 0]
    onehot = (targets[:, None] == jnp.arange(tile_count, dtype=jnp.int32)[None, :]).astype(
        jnp.int32
    )
    slot_rank = jnp.sum((jnp.cumsum(onehot, 0) - 1) * onehot, 1)
    slot_match = (
        slot_rank[None, None, :] == jnp.arange(CAP, dtype=jnp.int32)[None, :, None]
    ).astype(jnp.int32)
    chosen = onehot.T[:, None, :] * slot_match
    slot_index = jnp.sum(chosen * jnp.arange(tile_count, dtype=jnp.int32)[None, None, :], 2)
    filled = jnp.sum(chosen, 2) > 0
    buffer = jnp.take(strips, slot_index, axis=1)
    return jnp.where(filled[None, :, :, None, None], buffer, jnp.zeros((), jnp.float32))


def merge_strips(subimage, dest):
    received = lax.all_to_all(
        pack_strips(subimage, dest), "tile", split_axis=1, concat_axis=1, tiled=True
    )
    return jnp.sum(received, axis=(1, 2)) / math.sqrt(dest.shape[0])


def local(pulses, kernel, band_start, band_width, offset, owner, angle, dest):
    group_count = lax.axis_size("sub")
    own_block = pulses[0, 0]
    step_count = owner.shape[0]
    pulse_count = own_block.shape[1]
    window = kernel.shape[0]
    phase_gain = 1.0 / math.sqrt(pulse_count * step_count * group_count)
    depth = lax.broadcasted_iota(jnp.int32, kernel.shape, 0)
    in_band = (depth >= band_start) & (depth < band_start + band_width)
    masked = jnp.where(in_band, kernel, jnp.zeros((), kernel.dtype))
    rows_tile = angle.shape[3]
    subimage = jnp.zeros((2 * rows_tile, kernel.shape[1]), jnp.float32)
    for step in range(step_count):
        block_data = broadcast(own_block, "tile", owner[step])
        windowed = lax.dynamic_slice_in_dim(block_data, offset[0], window, 2).reshape(
            2 * pulse_count, window
        )
        interp = jnp.dot(windowed, masked, preferred_element_type=jnp.float32).astype(jnp.bfloat16)
        subimage = subimage + jnp.dot(
            phase_matrix(angle[0, step], phase_gain), interp, preferred_element_type=jnp.float32
        )
    subimage = lax.psum(subimage, "sub")
    merged = merge_strips(subimage, dest)
    return merged


def solution(mesh):
    placed = (
        P("sub", "tile", None, None, None),
        P("tile", None),
        P("tile", None),
        P("tile", None),
        P("tile"),
        P(),
        P("sub", None, None, "tile"),
        P("tile", None),
    )
    return jax.shard_map(
        local, mesh=mesh, in_specs=placed, out_specs=P(None, "tile", None), check_vma=False
    )
```

profile of v0, /device:TPU:1, one launch (start us, length us, event | category | flops | bytes accessed | tf_op | source)
XLA Modules:
  0.0 1269.9 jit_solution(12533749479444205495)
XLA Ops:
  6.5 1.6 fusion.124
  13.3 7.0 select_bitcast_fusion.1
  21.2 0.7 copy-done
  21.9 4.9 fusion.88
  26.8 8.6 fusion.96
  35.4 676.3 %all-reduce.6.cloned.1.call-done = (bf16[2,64,8192]{2,1,0:T(8,128)(2,1)}, bf16[2,64,8192]{2,1,0:T(8,128)(2,1)}, bf16[2,64,8192]{2,1,0:T(8,128)(2,1)}, bf16[2,64,...) async-done(((bf16[2,64,8192]{2,1,0:T(8,128)(2,1)}, ...) | async-done | bytes 16777232 | tf_op jit(solution)/shard_map/psum | solution.py:14
  711.7 3.8 constant_dynamic-slice_fusion.4
  715.6 3.7 constant_dynamic-slice_fusion.6
  719.2 1.8 constant_dynamic-slice_fusion.2
  721.0 0.8 constant_dynamic-slice_fusion
  721.8 11.8 fusion.5
  733.6 12.0 fusion.6
  745.6 11.8 fusion.7
  757.4 11.8 fusion.8
  769.1 12.0 fusion.4
  781.1 11.5 fusion.3
  792.6 11.5 fusion.2
  804.1 26.9 %add_add_fusion = f32[2048,1024]{1,0:T(8,128)} fusion(f32[2048,1024]{1,0:T(8,128)} %fusion.2, f32[2048,1024]{1,0:T(8,128)} %fusion.3, f32[2048,1024]{1,0:T(8,128)} %fusion.4, f32[2048,1024]{1,0:T(8,128)} %fusion.5, f32[2048,1024]{1,0:T(8,128)} %fusion.6, f32[2048,1024]{1,0:T(8,128)} %fusion.8, f32[2048,1024]{1,0:T(8,128)} %fusion.7, ...), kind=kOutput, calls=%fused_computation.6 | convolution fusion | flops 1644298240 | bytes 76947456 | tf_op jit(solution)/shard_map/dot_general | solution.py:68
  831.0 0.6 copy-done.6
  831.7 0.1 reduce_window_sum.11
  831.8 0.2 select_reduce_fusion
  832.0 0.2 multiply_reduce_fusion
  832.2 0.1 copy.17
  832.3 0.1 reshape.210
  832.4 0.1 copy.15
  832.5 0.1 copy.16
  832.7 204.1 %all-reduce.4.cloned.1.call-done = f32[2,64,16,1024]{3,2,1,0:T(8,128)} async-done(((f32[2,64,16,1024]{3,2,1,0:T(8,128)}), f32[2,64,16,1024]{3,2,1,0:T(8,128)}) %all-reduce.4.cloned.1.call-update) | async-done | bytes 8388624 | tf_op jit(solution)/shard_map/psum | solution.py:71
  1036.8 13.0 %gather_fusion = f32[128,2,16,1024]{3,2,1,0:T(8,128)} fusion(f32[2,64,16,1024]{3,2,1,0:T(8,128)} %all-reduce.4.cloned.1.call-done, s32[1024]{0:T(1024)S(1)} %pad_clamp_fusion), kind=kCustom, calls=%fused_computation | custom fusion | bytes 33554944 | tf_op jit(solution)/shard_map/jit(_take)/gather | solution.py:39
  1049.8 7.7 select_bitcast_fusion
  1057.6 197.9 %all_to_all.5 = f32[2,64,2,16,1024]{4,3,0,2,1:T(8,128)} all-to-all(f32[2,64,2,16,1024]{4,3,0,2,1:T(8,128)S(1)} %select_bitcast_fusion), channel_id=1, replica_groups=mesh['tile'=64,'sub'=2] {'tile'}, dimensions={1} | all-to-all | bytes 33554432 | tf_op jit(solution)/shard_map/all_to_all | solution.py:44
  1255.5 6.7 reduce_sum.42
  1262.2 0.7 broadcast_multiply_fusion
  (24 shorter events, 0.2 us)
Async XLA Ops:
  6.5 705.2 %all-reduce.6.cloned.1.call-start = ((), (), s32[]{:S(2)}) async-start(), calls=%async_computation.2 | async-start | bytes 33554432 | tf_op jit(solution)/shard_map/psum | solution.py:14
  20.3 0.9 copy-start.5
  20.3 0.9 copy-start.7
  20.3 1.6 copy-start
  20.3 1016.4 %all-reduce.4.cloned.1.call-start = ((), (), s32[]{:S(2)}) async-start(), calls=%async_computation.1 | async-start | bytes 16777216 | tf_op jit(solution)/shard_map/psum | solution.py:71
  711.7 7.5 copy-start.3
  711.7 7.5 copy-start.4
  711.7 9.3 copy-start.1
  711.7 9.3 copy-start.2
  831.0 0.7 copy-start.6
Sparse Core Ops, SparseCore 0:
  20.4 691.2 all-reduce.5
  831.1 205.5 all-reduce.3
where the time goes:
time: 1280 us; the launch traced here: 1270 us
  waiting for transfers between devices  880 us (69%)
  blocking collectives  198 us (15%)
  matrix products  109 us (9%)
  other arithmetic  36.2 us (3%)
  local copies, waits for them, and re-layouts  26.6 us (2%)
  between operations  19.7 us (2%)
    psum x1, waiting for transfers between devices, broadcast(): return lax.psum(block, axis)  676 us
    psum x1, waiting for transfers between devices, local(): subimage = lax.psum(subimage, 'sub')  204 us
    all_to_all x1, blocking collectives, merge_strips(): lax.all_to_all(pack_strips(subimage, dest), 'tile', split_axis=1, concat_...  198 us
    dot_general x8, matrix products, local(): jnp.dot(phase_matrix(angle[0, step], phase_gain), interp, preferred_eleme...  109 us
  transfers between devices with their start and end apart: 2, of which 2 were waited for; matrix products, arithmetic and copies ran while one was open for 1% of the time, Pallas kernels for 0%

commit v1 on v0

v1 whole, which is shorter than its diff:
```python
import math

import jax
import jax.numpy as jnp
from jax import lax
from jax.experimental import pallas as pl
from jax.experimental.pallas import tpu as pltpu
from jax.sharding import PartitionSpec as P

STRIP = 16
PAD = 256


def mate_of(count):
    return [(i, i ^ 1) for i in range(count)]


def fit_window(kernel, band_start, band_width, shift, rows):
    depth = lax.broadcasted_iota(jnp.int32, (rows, kernel.shape[1]), 0) - shift
    in_band = (depth >= band_start) & (depth < band_start + band_width)
    framed = lax.dynamic_slice_in_dim(
        jnp.pad(kernel, ((PAD, PAD), (0, 0))), PAD - shift, rows, 0
    )
    return jnp.where(in_band, framed, jnp.zeros((), kernel.dtype))


def phase_rows(angle, scale, core):
    steps, pulses, rows = angle.shape
    ordered = angle.reshape(steps, pulses // 2, 2, rows).transpose(2, 1, 0, 3)
    ordered = jnp.where(core == 0, ordered, ordered[::-1])
    cosine = (jnp.cos(ordered) * scale).astype(jnp.bfloat16)
    sine = (jnp.sin(ordered) * scale).astype(jnp.bfloat16)
    top = jnp.stack([cosine, -sine], 2).reshape(2 * steps * pulses, rows)
    low = jnp.stack([sine, cosine], 2).reshape(2 * steps * pulses, rows)
    return jnp.concatenate([top, low], 1).T


def interp_kernel(info, rows_ref, kernel_ref, keep_ref, send_ref, *, depth):
    half, tile = pl.program_id(0), pl.program_id(1)
    start = pl.multiple_of(info[1 + tile], 128)
    out = jnp.dot(
        rows_ref[:, pl.ds(start, depth)], kernel_ref[0], preferred_element_type=jnp.float32
    ).astype(jnp.bfloat16)

    @pl.when(half == 0)
    def _():
        keep_ref[...] = out

    @pl.when(half == 1)
    def _():
        send_ref[...] = out


def interpolate(info, rows, kernels):
    count, samples = rows.shape
    tiles, depth, columns = kernels.shape
    half = columns // 2
    block = 256
    parts = half // block
    out = jax.ShapeDtypeStruct((count, tiles * half), jnp.bfloat16)

    def kernel_at(h, t, n, info):
        return (t, 0, jnp.where(h == 0, info[0], 1 - info[0]) * parts + n)

    def keep_at(h, t, n, info):
        return (0, jnp.where(h == 0, t * parts + n, tiles * parts - 1))

    def send_at(h, t, n, info):
        return (0, jnp.where(h == 0, 0, t * parts + n))

    return pl.pallas_call(
        lambda *refs: interp_kernel(*refs, depth=depth),
        out_shape=(out, out),
        grid_spec=pltpu.PrefetchScalarGridSpec(
            num_scalar_prefetch=1,
            grid=(2, tiles, parts),
            in_specs=[
                pl.BlockSpec((count, samples), lambda h, t, n, info: (0, 0)),
                pl.BlockSpec((1, depth, block), kernel_at),
            ],
            out_specs=[
                pl.BlockSpec((count, block), keep_at),
                pl.BlockSpec((count, block), send_at),
            ],
        ),
        compiler_params=pltpu.CompilerParams(vmem_limit_bytes=56 << 20),
        cost_estimate=pl.CostEstimate(
            flops=2 * count * depth * tiles * columns,
            bytes_accessed=2 * (count * samples + tiles * depth * columns),
            transcendentals=0,
        ),
        name="interp",
    )(info, rows, kernels)


def image_kernel(dest, phase_ref, own_ref, mate_ref, out_ref, total_ref, *, steps):
    tile, part = pl.program_id(0), pl.program_id(1)
    half = out_ref.shape[1]
    near = own_ref.shape[0]
    block = phase_ref.shape[1]

    @pl.when((tile == 0) & (part == 0))
    def _():
        total_ref[...] = jnp.zeros_like(total_ref)

    def add(own_column, mate_column):
        image = jnp.dot(
            phase_ref[0, :, :near],
            own_ref[:, own_column : own_column + half],
            preferred_element_type=jnp.float32,
        ) + jnp.dot(
            phase_ref[0, :, near:],
            mate_ref[:, mate_column : mate_column + half],
            preferred_element_type=jnp.float32,
        )
        per_side = steps // 2
        side = part // per_side
        first = (part % per_side) * (block // STRIP)
        for strip in range(block // STRIP):
            target = dest[tile, first + strip]
            at = pl.multiple_of(target * (2 * STRIP) + side * STRIP, STRIP)
            total_ref[pl.ds(at, STRIP), :] += image[strip * STRIP : (strip + 1) * STRIP]

    @pl.when(tile == 0)
    def _():
        add(0, half)

    @pl.when(tile == 1)
    def _():
        add(half, 0)

    @pl.when((tile == 1) & (part == steps - 1))
    def _():
        out_ref[...] = total_ref[...].astype(out_ref.dtype)


def parent_sums(dest, phases, own, mate):
    tiles, rows, depth = phases.shape
    half = own.shape[1] // 2
    block = 512
    steps = rows // block
    return pl.pallas_call(
        lambda *refs: image_kernel(*refs, steps=steps),
        out_shape=jax.ShapeDtypeStruct((rows, half), jnp.bfloat16),
        grid_spec=pltpu.PrefetchScalarGridSpec(
            num_scalar_prefetch=1,
            grid=(tiles, steps),
            in_specs=[
                pl.BlockSpec((1, block, depth), lambda t, i, dest: (t, i, 0)),
                pl.BlockSpec(own.shape, lambda t, i, dest: (0, 0)),
                pl.BlockSpec(mate.shape, lambda t, i, dest: (0, 0)),
            ],
            out_specs=pl.BlockSpec((rows, half), lambda t, i, dest: (0, 0)),
            scratch_shapes=[pltpu.VMEM((rows, half), jnp.float32)],
        ),
        compiler_params=pltpu.CompilerParams(vmem_limit_bytes=48 << 20),
        cost_estimate=pl.CostEstimate(
            flops=2 * tiles * rows * depth * half,
            bytes_accessed=2 * (tiles * rows * depth + 2 * rows * half),
            transcendentals=0,
        ),
        name="image",
    )(dest, phases, own, mate)


def gather_rows(rows, tile_count):
    groups = [[t for t in range(tile_count) if t % 2 == c] for c in range(2)]
    return lax.all_gather(rows, "tile", axis=0, tiled=True, axis_index_groups=groups)


def local(pulses, kernel, band_start, band_width, offset, owner, angle, dest):
    groups = lax.axis_size("sub")
    tile_count = lax.axis_size("tile")
    core = lax.axis_index("tile") % 2
    mates = mate_of(tile_count)
    _, _, parts, pulse_count, samples = pulses.shape
    step_count = owner.shape[0]
    window, columns = kernel.shape
    depth = window + PAD
    scale = 1.0 / math.sqrt(pulse_count * step_count * groups)

    spread = lax.all_to_all(
        pulses[0, 0].transpose(1, 0, 2), "tile", split_axis=0, concat_axis=0, tiled=True
    )
    mine = jnp.take(spread, owner, axis=0).transpose(1, 0, 2).reshape(parts * step_count, samples)

    small = jnp.concatenate([band_start[0], band_width[0], dest[:, 0], offset])
    other_small = lax.ppermute(small, "tile", mates)
    other_kernel = lax.ppermute(kernel, "tile", mates)
    other_angle = lax.ppermute(angle[0], "tile", mates)

    rows = gather_rows(mine, tile_count)

    starts, framed, phases, dests = [], [], [], []
    for ints, weights, phase in ((small, kernel, angle[0]), (other_small, other_kernel, other_angle)):
        at = ints[-1]
        start = jnp.minimum(at // 128 * 128, samples - depth)
        starts.append(start)
        framed.append(
            fit_window(weights, ints[:columns][None], ints[columns : 2 * columns][None], at - start, depth)
        )
        phases.append(phase_rows(phase, scale, core))
        dests.append(ints[2 * columns : -1])
    info = jnp.stack([core, *starts]).astype(jnp.int32)

    keep, send = interpolate(info, rows, jnp.stack(framed))
    mate = lax.ppermute(send, "tile", mates)
    sums = parent_sums(jnp.stack(dests), jnp.stack(phases), keep, mate)

    received = lax.all_to_all(sums, ("tile", "sub"), split_axis=0, concat_axis=0, tiled=True)
    received = received.reshape(tile_count // 2, 2, groups, STRIP, columns // 2)
    side = jnp.sum(received.astype(jnp.float32), axis=(0, 2)) / math.sqrt(tile_count)
    side = side.transpose(1, 0, 2).reshape(STRIP, columns)
    other = lax.ppermute(side, "sub", [(0, 1), (1, 0)])
    first = lax.axis_index("sub") == 0
    return jnp.stack([jnp.where(first, side, other), jnp.where(first, other, side)])


def solution(mesh):
    placed = (
        P("sub", "tile", None, None, None),
        P("tile", None),
        P("tile", None),
        P("tile", None),
        P("tile"),
        P(),
        P("sub", None, None, "tile"),
        P("tile", None),
    )
    return jax.shard_map(
        local, mesh=mesh, in_specs=placed, out_specs=P(None, "tile", None), check_vma=False
    )
```

time: 1280 us -> 253 us (0.20)
  waiting for transfers between devices: 880 us -> 40.8 us
  blocking collectives: 198 us -> 36.3 us
  matrix products: 109 us -> 0 us
  other arithmetic: 36.2 us -> 79.6 us
  Pallas kernels: 0 us -> 28.3 us
  starting transfers between devices: 0.04 us -> 15.1 us
    psum x2 -> x0, waiting for transfers between devices: 880 us -> none  [the longest x1 676 us: broadcast(): return lax.psum(block, axis)]
    all_to_all x1, blocking collectives: 198 us -> 36.3 us  [local(): lax.all_to_all(sums, ('tile', 'sub'), split_axis=0, concat_axis=0, tiled=...]
    dot_general x8 -> x0, matrix products: 109 us -> none  [local(): jnp.dot(phase_matrix(angle[0, step], phase_gain), interp, preferred_eleme...]
    another operation x3 -> x17, other arithmetic: 13.6 us -> 78.9 us  [the longest x3 29.1 us: local(): keep, send = interpolate(info, rows, jnp.stack(framed))]
    all_to_all x0 -> x1, waiting for transfers between devices: none -> 30.4 us  [local(): lax.all_to_all(pulses[0, 0].transpose(1, 0, 2), 'tile', split_axis=0, con...]
    pallas_call x0 -> x2, Pallas kernels: none -> 28.3 us  [the longest x1 18.1 us: interpolate(): pl.pallas_call(lambda *refs: interp_kernel(*refs, depth=depth), out_shape...]
    reshape x0 -> x5, local copies, waits for them, and re-layouts: none -> 15.8 us  [the longest x2 7.91 us: phase_rows(): low = jnp.stack([sine, cosine], 2).reshape(2 * steps * pulses, rows)]
    select_n x3 -> x2, other arithmetic: 14.8 us -> 0.3 us  [local(): jnp.take(spread, owner, axis=0).transpose(1, 0, 2)]
  transfers between devices with their start and end apart: 2 -> 7, of which waited for: 2 -> 3; matrix products, arithmetic and copies ran while one was open for 1% -> 42% of each run, Pallas kernels for 0% -> 0%
where the time goes in v1:
time: 253 us; the launch traced here: 252 us
  other arithmetic  79.6 us (31%)
  waiting for transfers between devices  40.8 us (16%)
  blocking collectives  36.3 us (14%)
  local copies, waits for them, and re-layouts  34.1 us (13%)
  Pallas kernels  28.3 us (11%)
  between operations  17.5 us (7%)
  starting transfers between devices  15.1 us (6%)
    all_to_all x1, blocking collectives, local(): lax.all_to_all(sums, ('tile', 'sub'), split_axis=0, concat_axis=0, tiled=...  36.3 us
    all_to_all x1, waiting for transfers between devices, local(): lax.all_to_all(pulses[0, 0].transpose(1, 0, 2), 'tile', split_axis=0, con...  30.4 us
    another operation x3, other arithmetic, local(): keep, send = interpolate(info, rows, jnp.stack(framed))  29.1 us
    pallas_call x1, Pallas kernels, interpolate(): pl.pallas_call(lambda *refs: interp_kernel(*refs, depth=depth), out_shape...  18.1 us
    another operation x3, other arithmetic, phase_rows(): low = jnp.stack([sine, cosine], 2).reshape(2 * steps * pulses, rows)  17.1 us
    another operation x4, other arithmetic, phase_rows(): top = jnp.stack([cosine, -sine], 2).reshape(2 * steps * pulses, rows)  16.9 us
    another operation x4, other arithmetic, local(): sums = parent_sums(jnp.stack(dests), jnp.stack(phases), keep, mate)  14.6 us
    all_to_all x1, starting transfers between devices, local(): lax.all_to_all(pulses[0, 0].transpose(1, 0, 2), 'tile', split_axis=0, con...  12.6 us
  transfers between devices with their start and end apart: 7, of which 3 were waited for; matrix products, arithmetic and copies ran while one was open for 42% of the time, Pallas kernels for 0%

profile of v1, /device:TPU:1, one launch (start us, length us, event | category | flops | bytes accessed | tf_op | source)
XLA Modules:
  0.0 251.7 jit_solution(8735713494046466399)
XLA Ops:
  6.5 5.1 %copy.79 = bf16[1,1,2,64,8192]{4,2,3,1,0:T(2,128)(2,1)} copy(bf16[1,1,2,64,8192]{4,3,2,1,0:T(8,128)(2,1)} %param.8) | data formatting | bytes 4194304 | tf_op args[0]
  11.6 12.6 %all-to-all-start = ((bf16[64,2,8192]{2,1,0:T(2,128)(2,1)}), bf16[64,2,8192]{2,1,0:T(2,128)(2,1)S(1)}, u32[]{:S(2)}, u32[]{:S(2)}) async-start(bf16[64,2,8192]{2,1,0:T(2,128)(2,1)} %bitcast.67), calls=%async_computation | async-start | bytes 4194304 | tf_op jit(solution)/shard_map/all_to_all | solution.py:182
  24.4 30.4 %all-to-all-done = bf16[64,2,8192]{2,1,0:T(2,128)(2,1)S(1)} async-done(((bf16[64,2,8192]{2,1,0:T(2,128)(2,1)}), bf16[64,2,8192]{2,1,0:T(2,128)(2,1)S(1)}, u32[]{:S(2)}, u32[]{:S(2)}) %all-to-all-start) | async-done | bytes 2097184 | tf_op jit(solution)/shard_map/all_to_all | solution.py:182
  54.8 1.1 gather_fusion
  56.1 0.9 copy.80
  58.4 2.8 %copy.81 = f32[1,8,64,1024]{3,1,2,0:T(8,128)S(1)} copy(f32[1,8,64,1024]{3,2,1,0:T(8,128)} %param.14) | data formatting | bytes 4194304 | tf_op args[6]
  61.6 6.9 %negate_bitcast_fusion = bf16[2,32,1,8,1024]{4,3,0,1,2:T(8,128)(2,1)S(1)} fusion(f32[2,32,8,1024]{3,2,0,1:T(8,128)S(1)} %bitcast.76, pred[]{:T(512)S(6)} %eq.10), kind=kLoop, calls=%fused_computation.26 | loop fusion | flops 3145728 | bytes 3145729 | tf_op jit(solution)/shard_map/stack | solution.py:33
  68.5 7.6 %fusion.4 = (bf16[2,32,1,8,1024]{4,3,0,1,2:T(8,128)(2,1)S(1)}, bf16[2,32,1,8,1024]{4,3,0,1,2:T(8,128)(2,1)S(1)}) fusion(f32[2,32,8,1024]{3,2,0,1:T(8,128)S(1)} %bitcast.77, pred[]{:T(512)S(6)} %eq.10), kind=kLoop, calls=%fused_computation.34 | loop fusion | flops 2621440 | bytes 4194305 | tf_op jit(solution)/shard_map/stack | solution.py:34
  76.2 1.7 pad_maximum_fusion.2
  77.9 1.5 copy.55
  79.4 4.0 %copy.57 = bf16[1024,1024]{0,1:T(8,128)(2,1)} copy(bf16[1024,1024]{1,0:T(8,128)(2,1)} %bitcast.78) | data formatting | bytes 4194304 | tf_op jit(solution)/shard_map/reshape | solution.py:33
  83.4 3.1 %copy.56 = bf16[2,32,2,8,1024]{4,3,2,1,0:T(8,128)(2,1)} copy(bf16[2,32,2,8,1024]{4,3,0,1,2:T(8,128)(2,1)} %get-tuple-element.16) | data formatting | bytes 4194304 | tf_op jit(solution)/shard_map/stack | solution.py:34
  86.5 4.0 %copy.58 = bf16[1024,1024]{0,1:T(8,128)(2,1)} copy(bf16[1024,1024]{1,0:T(8,128)(2,1)} %bitcast.79) | data formatting | bytes 4194304 | tf_op jit(solution)/shard_map/reshape | solution.py:34
  90.5 10.0 %fusion = bf16[1,4352,1024]{2,1,0:T(8,128)(2,1)} fusion(s32[]{:T(128)S(6)} %select_n.74, bf16[4096,1024]{1,0:T(8,128)(2,1)} %param.9, s32[1024]{0:T(1024)S(1)} %bitcast.88, s32[1024]{0:T(1024)S(1)} %bitcast.87, s32[4352]{0:T(1024)S(1)} %iota_subtract_fusion.1), kind=kLoop, calls=%fused_computation.6 | loop fusion | flops 17825792 | bytes 17327108 | tf_op jit(solution)/shard_map/stack | solution.py:206
  100.5 2.4 maximum_bitcast_fusion
  107.4 9.2 %fusion.5 = (bf16[2,32,1,8,1024]{4,3,0,1,2:T(8,128)(2,1)S(1)}, bf16[2,32,8,1024]{3,2,0,1:T(8,128)(2,1)S(1)}) fusion(f32[2,32,8,1024]{3,2,0,1:T(8,128)} %bitcast.17, pred[]{:T(512)S(6)} %eq.10), kind=kLoop, calls=%fused_computation.35 | loop fusion | flops 2621440 | bytes 4194305 | tf_op jit(solution)/shard_map/stack | solution.py:34
  116.6 8.1 %copy_bitcast_fusion.1 = (bf16[2,32,1,8,1024]{4,3,1,0,2:T(8,128)(2,1)S(1)}, bf16[2,32,1,8,1024]{4,3,1,0,2:T(8,128)(2,1)S(1)}) fusion(bf16[2,32,8,1024]{3,2,0,1:T(8,128)(2,1)S(1)} %get-tuple-element.14, f32[2,32,8,1024]{3,2,0,1:T(8,128)} %bitcast.17, pred[]{:T(512)S(6)} %eq.10), kind=kLoop, calls=%fused_computation.24 | loop fusion | flops 3145728 | bytes 5242881 | tf_op jit(solution)/shard_map/stack | solution.py:33
  124.9 1.6 copy.62
  126.5 3.9 %copy.65 = bf16[1024,1024]{0,1:T(8,128)(2,1)} copy(bf16[1024,1024]{1,0:T(8,128)(2,1)} %bitcast.80) | data formatting | bytes 4194304 | tf_op jit(solution)/shard_map/reshape | solution.py:33
  130.4 7.5 %fusion.1 = bf16[1,4352,1024]{2,1,0:T(8,128)(2,1)S(1)} fusion(s32[]{:T(128)S(6)} %select_n.76, bf16[4096,1024]{1,0:T(8,128)(2,1)} %collective-permute-done.2, s32[1024]{0:T(1024)S(1)} %get-tuple-element.20, s32[1024]{0:T(1024)S(1)} %get-tuple-element.19, s32[4352]{0:T(1024)S(1)} %iota_subtract_fusion), kind=kLoop, calls=%fused_computation.7 | loop fusion | flops 17825792 | bytes 17327108 | tf_op jit(solution)/shard_map/stack | solution.py:206
  137.9 11.6 %pad_maximum_fusion.refs_2_ = bf16[2,4352,1024]{2,1,0:T(8,128)(2,1)} fusion(bf16[1,4352,1024]{2,1,0:T(8,128)(2,1)S(1)} %fusion.1, bf16[1,4352,1024]{2,1,0:T(8,128)(2,1)} %fusion), kind=kLoop, calls=%fused_computation.1 | loop fusion | flops 8912896 | bytes 35651584 | tf_op jit(solution)/shard_map/stack | solution.py:206
  149.5 7.3 %all-gather.2.cloned.1.call-done.refs_1_ = bf16[512,8192]{1,0:T(8,128)(2,1)} async-done(((bf16[16,8192]{1,0:T(8,128)(2,1)}), bf16[512,8192]{1,0:T(8,128)(2,1)}) %all-gather.2.cloned.1.call-update) | async-done | bytes 8388624 | tf_op jit(solution)/shard_map/all_gather | solution.py:168
  156.8 18.1 %interp.1 = (bf16[512,1024]{1,0:T(8,128)(2,1)}, bf16[512,1024]{1,0:T(8,128)(2,1)}) custom-call(s32[3]{0:T(128)} %pad_add_fusion.1.refs_0_, bf16[512,8192]{1,0:T(8,128)(2,1)} %all-gather.2.cloned.1.call-done.refs_1_, bf16[2,4352,1024]{2,1,0:T(8,128)(2,1)} %pad_maximum_fusion.refs_2_), custom_call_target="tpu_custom_call" | custom-call | flops 9126805504 | bytes 26214400 | tf_op jit(solution)/shard_map/interp/pallas_call | solution.py:71
  174.8 1.1 collective-permute-start.3
  176.1 1.5 copy.64
  177.6 4.0 %copy.66 = bf16[1024,1024]{0,1:T(8,128)(2,1)} copy(bf16[1024,1024]{1,0:T(8,128)(2,1)} %bitcast.81) | data formatting | bytes 4194304 | tf_op jit(solution)/shard_map/reshape | solution.py:34
  181.5 4.6 %maximum_bitcast_fusion.1 = bf16[1,2048,1024]{2,1,0:T(8,128)(2,1)} fusion(bf16[1024,1024]{0,1:T(8,128)(2,1)} %copy.66, bf16[1024,1024]{0,1:T(8,128)(2,1)} %copy.65), kind=kLoop, calls=%fused_computation.10 | loop fusion | flops 8388608 | bytes 8388608 | tf_op jit(solution)/shard_map/stack | solution.py:208
  186.2 7.5 %pad_maximum_fusion.1.refs_1_ = bf16[2,2048,1024]{2,1,0:T(8,128)(2,1)} fusion(bf16[1,2048,1024]{2,1,0:T(8,128)(2,1)} %maximum_bitcast_fusion.1, bf16[1,2048,1024]{2,1,0:T(8,128)(2,1)} %maximum_bitcast_fusion), kind=kLoop, calls=%fused_computation.8 | loop fusion | flops 4194304 | bytes 16777216 | tf_op jit(solution)/shard_map/stack | solution.py:208
  193.7 10.3 %image.1 = bf16[2048,512]{1,0:T(8,128)(2,1)S(1)} custom-call(s32[2,64]{1,0:T(2,128)S(1)} %pad_add_fusion.refs_0_, bf16[2,2048,1024]{2,1,0:T(8,128)(2,1)} %pad_maximum_fusion.1.refs_1_, bf16[512,1024]{1,0:T(8,128)(2,1)S(1)} %copy-done, bf16[512,1024]{1,0:T(8,128)(2,1)S(1)} %collective-permute-done.3.refs_3_), custom_call_target="tpu_custom_call" | custom-call | flops 4294967296 | bytes 12582912 | tf_op jit(solution)/shard_map/image/pallas_call | solution.py:142
  204.0 36.3 %all_to_all.14 = bf16[128,16,512]{2,1,0:T(8,128)(2,1)S(1)} all-to-all(bf16[128,16,512]{2,1,0:T(8,128)(2,1)S(1)} %bitcast.74), channel_id=1, replica_groups=mesh['tile'=64,'sub'=2] {'tile','sub'}, dimensions={0} | all-to-all | bytes 4194304 | tf_op jit(solution)/shard_map/all_to_all | solution.py:210
  241.1 3.1 %collective-permute-done.4 = f32[16,1024]{1,0:T(8,128)S(1)} collective-permute-done((f32[16,1024]{1,0:T(8,128)S(1)}, f32[16,1024]{1,0:T(8,128)S(1)}, u32[]{:S(2)}, u32[]{:S(2)}) %collective-permute-start.4) | collective-permute-done | bytes 65568 | tf_op jit(solution)/shard_map/ppermute | solution.py:214
  244.2 0.7 pad_maximum_fusion.6
  (43 shorter events, 4.0 us)
Async XLA Ops:
  11.6 12.7 %copy-start.6 = (s32[8]{0:T(128)S(1)}, s32[8]{0:T(128)}, u32[]{:S(2)}) copy-start(s32[8]{0:T(128)} %param.13) | copy-start | bytes 100
  11.6 46.3 %copy-start.3 = (s32[1,1024]{1,0:T(1,128)S(1)}, s32[1,1024]{1,0:T(1,128)}, u32[]{:S(2)}) copy-start(s32[1,1024]{1,0:T(1,128)} %param.10) | copy-start | bytes 12292
  11.6 46.3 %copy-start.4 = (s32[1,1024]{1,0:T(1,128)S(1)}, s32[1,1024]{1,0:T(1,128)}, u32[]{:S(2)}) copy-start(s32[1,1024]{1,0:T(1,128)} %param.11) | copy-start | bytes 12292
  11.6 46.3 %copy-start.5 = (s32[64,1]{0,1:T(1,128)S(1)}, s32[64,1]{0,1:T(1,128)}, u32[]{:S(2)}) copy-start(s32[64,1]{0,1:T(1,128)} %param.15) | copy-start | bytes 772
  11.6 43.1 %all-to-all-start = ((bf16[64,2,8192]{2,1,0:T(2,128)(2,1)}), bf16[64,2,8192]{2,1,0:T(2,128)(2,1)S(1)}, u32[]{:S(2)}, u32[]{:S(2)}) async-start(bf16[64,2,8192]{2,1,0:T(2,128)(2,1)} %bitcast.67), calls=%async_computation | async-start | bytes 4194304 | tf_op jit(solution)/shard_map/all_to_all | solution.py:182
  24.3 132.5 %all-gather.2.cloned.1.call-start = ((), (), s32[]{:S(2)}) async-start(), calls=%async_computation.2 | async-start | bytes 8650752 | tf_op jit(solution)/shard_map/all_gather | solution.py:168
  57.0 73.4 %collective-permute-start.2 = (bf16[4096,1024]{1,0:T(8,128)(2,1)}, bf16[4096,1024]{1,0:T(8,128)(2,1)}, u32[]{:S(2)}, u32[]{:S(2)}) collective-permute-start(bf16[4096,1024]{1,0:T(8,128)(2,1)} %param.9), channel_id=1, source_target_pairs={{0,2},{2,0},{4,6},{6,4},{8,10},{10,8},{12,14},{14,12},{16,18},{18,... | collective-permute-start | bytes 25165832 | tf_op jit(solution)/shard_map/ppermute | solution.py:189
  58.0 44.9 %collective-permute-start = (s32[2113]{0:T(1024)S(1)}, s32[2113]{0:T(1024)S(1)}, u32[]{:S(2)}, u32[]{:S(2)}) collective-permute-start(s32[2113]{0:T(1024)S(1)} %concatenate.9), channel_id=1, source_target_pairs={{0,2},{2,0},{4,6},{6,4},{8,10},{10,8},{12,14},{14,12},{16,18},{18,... | collective-permute-start | bytes 25364 | tf_op jit(solution)/shard_map/ppermute | solution.py:188
  61.2 46.2 %collective-permute-start.1 = (f32[8,64,1024]{2,0,1:T(8,128)S(1)}, f32[8,64,1024]{2,0,1:T(8,128)}, u32[]{:S(2)}, u32[]{:S(2)}) collective-permute-start(f32[8,64,1024]{2,0,1:T(8,128)S(1)} %bitcast.75), channel_id=1, source_target_pairs={{0,2},{2,0},{4,6},{6,4},{8,10},{10,8},{12,14},{14,12},{16,18},{18,... | collective-permute-start | bytes 6291464 | tf_op jit(solution)/shard_map/ppermute | solution.py:190
  90.5 10.0 %copy-start.1 = (bf16[1024,1024]{0,1:T(8,128)(2,1)S(1)}, bf16[1024,1024]{0,1:T(8,128)(2,1)}, u32[]{:S(2)}) copy-start(bf16[1024,1024]{0,1:T(8,128)(2,1)} %copy.57) | copy-start | bytes 6291460
  90.5 10.0 %copy-start.2 = (bf16[1024,1024]{0,1:T(8,128)(2,1)S(1)}, bf16[1024,1024]{0,1:T(8,128)(2,1)}, u32[]{:S(2)}) copy-start(bf16[1024,1024]{0,1:T(8,128)(2,1)} %copy.58) | copy-start | bytes 6291460
  174.8 18.9 %collective-permute-start.3 = (bf16[512,1024]{1,0:T(8,128)(2,1)}, bf16[512,1024]{1,0:T(8,128)(2,1)S(1)}, u32[]{:S(2)}, u32[]{:S(2)}) collective-permute-start(bf16[512,1024]{1,0:T(8,128)(2,1)} %get-tuple-element.8), channel_id=1, source_target_pairs={{0,2},{2,0},{4,6},{6,4},{8,10},{10,8},{12,14},{14,12},{16,18},{18,... | collective-permute-start | bytes 3145736 | tf_op jit(solution)/shard_map/ppermute | solution.py:207
  186.2 7.6 %copy-start = (bf16[512,1024]{1,0:T(8,128)(2,1)S(1)}, bf16[512,1024]{1,0:T(8,128)(2,1)}, u32[]{:S(2)}) copy-start(bf16[512,1024]{1,0:T(8,128)(2,1)} %get-tuple-element.7.refs_2_) | copy-start | bytes 3145732
  240.6 3.6 %collective-permute-start.4 = (f32[16,1024]{1,0:T(8,128)S(1)}, f32[16,1024]{1,0:T(8,128)S(1)}, u32[]{:S(2)}, u32[]{:S(2)}) collective-permute-start(f32[16,1024]{1,0:T(8,128)S(1)} %bitcast.84), channel_id=1, source_target_pairs={{0,1},{1,0},{2,3},{3,2},{4,5},{5,4},{6,7},{7,6},{8,9},{9,8},{10,11... | collective-permute-start | bytes 196616 | tf_op jit(solution)/shard_map/ppermute | solution.py:214
Sparse Core Ops, SparseCore 0:
  57.1 99.5 all-gather.1

commit v2 on v0

v2 whole, which is shorter than its diff:
```python
import math

import jax
import jax.numpy as jnp
from jax import lax
from jax.experimental import pallas as pl
from jax.experimental.pallas import tpu as pltpu
from jax.sharding import PartitionSpec as P

STRIP = 16
PAD = 256
SIDES = (4, 2, 4, 2)
MIB = 1 << 20
RING = (0, -1, 1, 2)


def tile_at(x, y, z, core):
    return (((x % SIDES[0]) * SIDES[1] + y % SIDES[1]) * SIDES[2] + z % SIDES[2]) * SIDES[3] + core


def shifted(dx=0, dy=0, dz=0):
    return [
        (tile_at(x, y, z, c), tile_at(x + dx, y + dy, z + dz, c))
        for x in range(SIDES[0])
        for y in range(SIDES[1])
        for z in range(SIDES[2])
        for c in range(SIDES[3])
    ]


def mates():
    count = math.prod(SIDES)
    return [(i, i ^ 1) for i in range(count)]


def ring_of_blocks(block, up, down):
    half = block.shape[1] // 2
    below = lax.ppermute(block, "tile", up)
    above = lax.ppermute(block, "tile", down)
    far_left = lax.ppermute(below[:, :half], "tile", up)
    far_right = lax.ppermute(above[:, half:], "tile", down)
    return jnp.concatenate([block, below, above, jnp.concatenate([far_left, far_right], 1)], 0)


def ring_of_lines(line, up, down):
    half = line.shape[0] // 2
    below = lax.ppermute(line, "tile", up)
    above = lax.ppermute(line, "tile", down)
    far_top = lax.ppermute(below[:half], "tile", up)
    far_low = lax.ppermute(above[half:], "tile", down)
    return [line, below, above], [far_top, far_low]


def gather_rows(mine):
    up_x, down_x, up_z, down_z = shifted(dx=1), shifted(dx=-1), shifted(dz=1), shifted(dz=-1)
    other = lax.ppermute(mine, "tile", shifted(dy=1))
    line_a = ring_of_blocks(mine, up_x, down_x)
    line_b = ring_of_blocks(other, up_z, down_z)
    first_a, last_a = ring_of_lines(line_a, up_z, down_z)
    first_b, last_b = ring_of_lines(line_b, up_x, down_x)
    return first_a + first_b, last_a + last_b


def block_order():
    first, last = [], []
    for dy in (0, 1):
        lines = [[(a, dy, b) if dy == 0 else (b, dy, a) for a in RING] for b in RING]
        first += lines[0] + lines[1] + lines[2]
        last += lines[3]
    return first + last


def frame_kernel(info, band_ref, before_ref, now_ref, out_ref):
    step = pl.program_id(0)
    shift = info[0]
    rows, columns = out_ref.shape
    source = lax.broadcasted_iota(jnp.int32, (rows, 2 * rows), 1)
    target = lax.broadcasted_iota(jnp.int32, (rows, 2 * rows), 0)
    move = jnp.where(source == target + (rows - shift), 1.0, 0.0).astype(jnp.bfloat16)
    moved = jnp.dot(move[:, :rows], before_ref[...], preferred_element_type=jnp.float32)
    moved += jnp.dot(move[:, rows:], now_ref[...], preferred_element_type=jnp.float32)
    depth = lax.broadcasted_iota(jnp.int32, (rows, columns), 0) + (step * rows - shift)
    low, high = band_ref[0:1, :], band_ref[1:2, :]
    out_ref[...] = jnp.where((depth >= low) & (depth < high), moved, 0.0).astype(out_ref.dtype)


def fit_window(shift, bands, kernel):
    window, columns = kernel.shape
    count = window // PAD
    rows = window + PAD
    return pl.pallas_call(
        frame_kernel,
        out_shape=jax.ShapeDtypeStruct((rows, columns), kernel.dtype),
        grid_spec=pltpu.PrefetchScalarGridSpec(
            num_scalar_prefetch=1,
            grid=(count + 1,),
            in_specs=[
                pl.BlockSpec((2, columns), lambda i, info: (0, 0)),
                pl.BlockSpec((PAD, columns), lambda i, info: (jnp.maximum(i - 1, 0), 0)),
                pl.BlockSpec((PAD, columns), lambda i, info: (jnp.minimum(i, count - 1), 0)),
            ],
            out_specs=pl.BlockSpec((PAD, columns), lambda i, info: (i, 0)),
        ),
        compiler_params=pltpu.CompilerParams(vmem_limit_bytes=24 * MIB),
        cost_estimate=pl.CostEstimate(
            flops=4 * rows * PAD * columns, bytes_accessed=6 * rows * columns, transcendentals=0
        ),
        name="frame",
    )(shift, bands, kernel, kernel)


def sine_cosine(angle):
    half = angle * 0.5
    square = half * half
    sine, cosine = jnp.float32(-1.0 / math.factorial(11)), jnp.float32(1.0 / math.factorial(12))
    for power in (9, 7, 5, 3, 1):
        sine = sine * square + jnp.float32((-1) ** (power // 2) / math.factorial(power))
    for power in (10, 8, 6, 4, 2, 0):
        cosine = cosine * square + jnp.float32((-1) ** (power // 2) / math.factorial(power))
    sine = sine * half
    return 2.0 * sine * cosine, 1.0 - 2.0 * sine * sine


def phase_kernel(order, angle_ref, out_ref, *, scale):
    pulses, steps, rows = angle_ref.shape
    group = 128 // steps
    for block in range(pulses // group):
        picked = [angle_ref[order[block * group + i]] for i in range(group)]
        sine, cosine = sine_cosine(jnp.concatenate(picked, 0))
        at = block * 128
        out_ref[:, at : at + 128] = (cosine * scale).T.astype(out_ref.dtype)
        at += pulses * steps
        out_ref[:, at : at + 128] = (sine * scale).T.astype(out_ref.dtype)


def phase_rows(order, angle, scale):
    pulses, steps, rows = angle.shape
    depth = 2 * pulses * steps
    block = 128
    return pl.pallas_call(
        lambda *refs: phase_kernel(*refs, scale=scale),
        out_shape=jax.ShapeDtypeStruct((rows, depth), jnp.bfloat16),
        grid_spec=pltpu.PrefetchScalarGridSpec(
            num_scalar_prefetch=1,
            grid=(rows // block,),
            in_specs=[pl.BlockSpec((pulses, steps, block), lambda i, order: (0, 0, i))],
            out_specs=pl.BlockSpec((block, depth), lambda i, order: (i, 0)),
        ),
        compiler_params=pltpu.CompilerParams(vmem_limit_bytes=24 * MIB),
        cost_estimate=pl.CostEstimate(
            flops=20 * depth * rows, bytes_accessed=4 * depth * rows, transcendentals=0
        ),
        name="phases",
    )(order, angle)


def interp_kernel(info, *refs, depth, pieces):
    parts, own_ref, mate_ref = refs[:pieces], refs[pieces], refs[pieces + 1]
    keep_ref, send_ref, rows_ref, sems = refs[pieces + 2 :]
    tile, half, part = pl.program_id(0), pl.program_id(1), pl.program_id(2)
    count = rows_ref.shape[0]

    @pl.when((tile == 0) & (half == 0) & (part == 0))
    def _():
        copies, at = [], 0
        for i, piece in enumerate(parts):
            size = piece.shape[0]
            copies.append(pltpu.make_async_copy(piece, rows_ref.at[pl.ds(at, size)], sems.at[i]))
            at += size
        for copy in copies:
            copy.start()
        for copy in copies:
            copy.wait()

    def work(kernel_ref):
        start = pl.multiple_of(info[1 + tile], 128)
        out = jnp.dot(
            rows_ref[:, pl.ds(start, depth)], kernel_ref[...], preferred_element_type=jnp.float32
        )
        out = out.reshape(count // 16, 2, 8, out.shape[1])
        real = out[:, 0].reshape(count // 2, -1).astype(jnp.bfloat16)
        imag = out[:, 1].reshape(count // 2, -1).astype(jnp.bfloat16)

        @pl.when(half == 0)
        def _():
            keep_ref[0] = real
            keep_ref[1] = imag

        @pl.when(half == 1)
        def _():
            send_ref[0] = real
            send_ref[1] = imag

    @pl.when(tile == 0)
    def _():
        work(own_ref)

    @pl.when(tile == 1)
    def _():
        work(mate_ref)


def interpolate(info, pieces, own, mate):
    count = sum(piece.shape[0] for piece in pieces)
    samples = pieces[0].shape[1]
    depth, columns = own.shape
    half = columns // 2
    block = 256
    parts = half // block
    out = jax.ShapeDtypeStruct((2, count // 2, 2 * half), jnp.bfloat16)

    def column(h, n, info):
        return jnp.where(h == 0, info[0], 1 - info[0]) * parts + n

    def own_at(t, h, n, info):
        return (0, jnp.where(t == 0, column(h, n, info), column(1, parts - 1, info)))

    def mate_at(t, h, n, info):
        return (0, jnp.where(t == 1, column(h, n, info), column(0, 0, info)))

    def keep_at(t, h, n, info):
        return (0, 0, t * parts + jnp.where(h == 0, n, parts - 1))

    def send_at(t, h, n, info):
        return (0, 0, jnp.where(h == 1, t * parts + n, jnp.maximum(t * parts - 1, 0)))

    return pl.pallas_call(
        lambda *refs: interp_kernel(*refs, depth=depth, pieces=len(pieces)),
        out_shape=(out, out),
        grid_spec=pltpu.PrefetchScalarGridSpec(
            num_scalar_prefetch=1,
            grid=(2, 2, parts),
            in_specs=[pl.BlockSpec(memory_space=pl.ANY) for _ in pieces]
            + [pl.BlockSpec((depth, block), own_at), pl.BlockSpec((depth, block), mate_at)],
            out_specs=[
                pl.BlockSpec((2, count // 2, block), keep_at),
                pl.BlockSpec((2, count // 2, block), send_at),
            ],
            scratch_shapes=[
                pltpu.VMEM((count, samples), jnp.bfloat16),
                pltpu.SemaphoreType.DMA((len(pieces),)),
            ],
        ),
        compiler_params=pltpu.CompilerParams(vmem_limit_bytes=40 * MIB),
        cost_estimate=pl.CostEstimate(
            flops=4 * count * depth * columns,
            bytes_accessed=2 * (count * samples + 2 * depth * columns),
            transcendentals=0,
        ),
        name="interp",
    )(info, *pieces, own, mate)


def image_kernel(info, dest, own_phase, mate_phase, *refs, steps):
    kept, taken, (out_ref, rhs_ref, total_ref) = refs[:2], refs[2:4], refs[4:]
    tile, part = pl.program_id(0), pl.program_id(1)
    half = out_ref.shape[1]
    depth = rhs_ref.shape[0]
    core = info[0]

    @pl.when((tile == 0) & (part == 0))
    def _():
        total_ref[...] = jnp.zeros_like(total_ref)

    def lay(pieces, cores_at, column):
        at = 0
        for piece in pieces:
            size = piece.shape[1]
            real = piece[0, :, column : column + half]
            imag = piece[1, :, column : column + half]
            cos_rows = pl.ds(pl.multiple_of(cores_at * (depth // 4) + at, 16), size)
            sin_rows = pl.ds(pl.multiple_of(cores_at * (depth // 4) + at + depth // 2, 16), size)
            rhs_ref[cos_rows, :half] = real
            rhs_ref[sin_rows, :half] = -imag
            rhs_ref[cos_rows, half:] = imag
            rhs_ref[sin_rows, half:] = real
            at += size

    @pl.when((tile == 0) & (part == 0))
    def _():
        lay(kept, core, 0)
        lay(taken, 1 - core, half)

    @pl.when((tile == 1) & (part == 0))
    def _():
        lay(kept, core, half)
        lay(taken, 1 - core, 0)

    def add(phase_ref):
        image = jnp.dot(phase_ref[...], rhs_ref[...], preferred_element_type=jnp.float32)
        block = image.shape[0]
        for strip in range(block // STRIP):
            target = dest[tile, part * (block // STRIP) + strip]
            at = pl.multiple_of(target * (2 * STRIP), 2 * STRIP)
            rows = slice(strip * STRIP, (strip + 1) * STRIP)
            total_ref[pl.ds(at, STRIP), :] += image[rows, :half]
            total_ref[pl.ds(at + STRIP, STRIP), :] += image[rows, half:]

    @pl.when(tile == 0)
    def _():
        add(own_phase)

    @pl.when(tile == 1)
    def _():
        add(mate_phase)

    @pl.when((tile == 1) & (part == steps - 1))
    def _():
        out_ref[...] = total_ref[...].astype(out_ref.dtype)


def parent_sums(info, dest, own_phase, mate_phase, kept, taken):
    rows, depth = own_phase.shape
    half = kept[0].shape[2] // 2
    block = 256
    steps = rows // block
    out_rows = 2 * rows

    def whole(array):
        return pl.BlockSpec(array.shape, lambda t, i, info, dest: (0,) * array.ndim)

    return pl.pallas_call(
        lambda *refs: image_kernel(*refs, steps=steps),
        out_shape=jax.ShapeDtypeStruct((out_rows, half), jnp.bfloat16),
        grid_spec=pltpu.PrefetchScalarGridSpec(
            num_scalar_prefetch=2,
            grid=(2, steps),
            in_specs=[
                pl.BlockSpec(
                    (block, depth), lambda t, i, info, dest: (jnp.where(t == 0, i, steps - 1), 0)
                ),
                pl.BlockSpec((block, depth), lambda t, i, info, dest: (jnp.where(t == 1, i, 0), 0)),
                *[whole(array) for array in (*kept, *taken)],
            ],
            out_specs=pl.BlockSpec((out_rows, half), lambda t, i, info, dest: (0, 0)),
            scratch_shapes=[
                pltpu.VMEM((depth, 2 * half), jnp.bfloat16),
                pltpu.VMEM((out_rows, half), jnp.float32),
            ],
        ),
        compiler_params=pltpu.CompilerParams(vmem_limit_bytes=40 * MIB),
        cost_estimate=pl.CostEstimate(
            flops=8 * rows * depth * half,
            bytes_accessed=4 * rows * depth + 8 * rows * half,
            transcendentals=0,
        ),
        name="image",
    )(info, dest, own_phase, mate_phase, *kept, *taken)


def local(pulses, kernel, band_start, band_width, offset, owner, angle, dest):
    groups = lax.axis_size("sub")
    tile_count = lax.axis_size("tile")
    me = lax.axis_index("tile")
    core = me % SIDES[3]
    _, _, parts, pulse_count, samples = pulses.shape
    step_count = owner.shape[0]
    window, columns = kernel.shape
    depth = window + PAD
    scale = 1.0 / math.sqrt(pulse_count * step_count * groups)

    spread = lax.all_to_all(
        pulses[0, 0].transpose(1, 0, 2), "tile", split_axis=0, concat_axis=0, tiled=True
    )
    mine = jnp.take(spread, owner, axis=0).transpose(1, 0, 2).reshape(parts * step_count, samples)
    first, last = gather_rows(mine)

    start = jnp.minimum(offset[0] // 128 * 128, samples - depth)
    bands = jnp.concatenate([band_start, band_start + band_width], 0)
    own_kernel = fit_window((offset - start).astype(jnp.int32), bands, kernel)
    x, y, z = me // (SIDES[1] * SIDES[2] * SIDES[3]), me // (SIDES[2] * SIDES[3]), me // SIDES[3]
    order = jnp.stack(
        [tile_at(x + dx, y + dy, z + dz, c) for c in range(SIDES[3]) for dx, dy, dz in block_order()]
    ).astype(jnp.int32)
    own_phase = phase_rows(order, angle[0].transpose(1, 0, 2), scale)
    ints = jnp.concatenate([dest[:, 0], start[None]])
    mate_ints = lax.ppermute(ints, "tile", mates())
    mate_kernel = lax.ppermute(own_kernel, "tile", mates())
    mate_phase = lax.ppermute(own_phase, "tile", mates())
    info = jnp.stack([core, ints[-1], mate_ints[-1]]).astype(jnp.int32)
    dests = jnp.stack([ints[:-1], mate_ints[:-1]])

    kept, taken = [], []
    for pieces in (first, last):
        keep, send = interpolate(info, pieces, own_kernel, mate_kernel)
        kept.append(keep)
        taken.append(lax.ppermute(send, "tile", mates()))
    sums = parent_sums(info, dests, own_phase, mate_phase, kept, taken)

    received = lax.all_to_all(sums, ("tile", "sub"), split_axis=0, concat_axis=0, tiled=True)
    received = received.reshape(tile_count // 2, 2, groups, STRIP, columns // 2)
    side = jnp.sum(received.astype(jnp.float32), axis=(0, 2)) / math.sqrt(tile_count)
    side = side.transpose(1, 0, 2).reshape(STRIP, columns)
    other = lax.ppermute(side, "sub", [(0, 1), (1, 0)])
    first_sub = lax.axis_index("sub") == 0
    return jnp.stack([jnp.where(first_sub, side, other), jnp.where(first_sub, other, side)])


def solution(mesh):
    placed = (
        P("sub", "tile", None, None, None),
        P("tile", None),
        P("tile", None),
        P("tile", None),
        P("tile"),
        P(),
        P("sub", None, None, "tile"),
        P("tile", None),
    )
    return jax.shard_map(
        local, mesh=mesh, in_specs=placed, out_specs=P(None, "tile", None), check_vma=False
    )
```

time: 1280 us -> 206 us (0.16)
  waiting for transfers between devices: 880 us -> 57.5 us
  blocking collectives: 198 us -> 34.1 us
  matrix products: 109 us -> 0 us
  Pallas kernels: 0 us -> 53.7 us
  starting transfers between devices: 0.04 us -> 37.9 us
  other arithmetic: 36.2 us -> 4.66 us
  between operations: 19.7 us -> 0.96 us
    psum x2 -> x0, waiting for transfers between devices: 880 us -> none  [the longest x1 676 us: broadcast(): return lax.psum(block, axis)]
    all_to_all x1, blocking collectives: 198 us -> 34.1 us  [local(): lax.all_to_all(sums, ('tile', 'sub'), split_axis=0, concat_axis=0, tiled=...]
    dot_general x8 -> x0, matrix products: 109 us -> none  [local(): jnp.dot(phase_matrix(angle[0, step], phase_gain), interp, preferred_eleme...]
    pallas_call x0 -> x5, Pallas kernels: none -> 53.7 us  [the longest x2 27.4 us: interpolate(): pl.pallas_call(lambda *refs: interp_kernel(*refs, depth=depth, pieces=len...]
    all_to_all x0 -> x1, waiting for transfers between devices: none -> 30.4 us  [local(): lax.all_to_all(pulses[0, 0].transpose(1, 0, 2), 'tile', split_axis=0, con...]
    ppermute x0 -> x23, waiting for transfers between devices: none -> 27 us  [the longest x2 10 us: ring_of_lines(): below = lax.ppermute(line, 'tile', up)]
    ppermute x0 -> x23, starting transfers between devices: none -> 26.5 us  [the longest x2 5.08 us: ring_of_lines(): far_low = lax.ppermute(above[half:], 'tile', down)]
    select_n x3 -> x2, other arithmetic: 14.8 us -> 0.3 us  [local(): jnp.take(spread, owner, axis=0).transpose(1, 0, 2)]
  transfers between devices with their start and end apart: 2 -> 24, of which waited for: 2 -> 7; matrix products, arithmetic and copies ran while one was open for 1% -> 7% of each run, Pallas kernels for 0% -> 16%
where the time goes in v2:
time: 206 us; the launch traced here: 205 us
  waiting for transfers between devices  57.5 us (28%)
  Pallas kernels  53.7 us (26%)
  starting transfers between devices  37.9 us (18%)
  blocking collectives  34.1 us (17%)
  local copies, waits for them, and re-layouts  16 us (8%)
  other arithmetic  4.66 us (2%)
    all_to_all x1, blocking collectives, local(): lax.all_to_all(sums, ('tile', 'sub'), split_axis=0, concat_axis=0, tiled=...  34.1 us
    all_to_all x1, waiting for transfers between devices, local(): lax.all_to_all(pulses[0, 0].transpose(1, 0, 2), 'tile', split_axis=0, con...  30.4 us
    pallas_call x2, Pallas kernels, interpolate(): pl.pallas_call(lambda *refs: interp_kernel(*refs, depth=depth, pieces=len...  27.4 us
    pallas_call x1, Pallas kernels, fit_window(): pl.pallas_call(frame_kernel, out_shape=jax.ShapeDtypeStruct((rows, column...  11.5 us
    all_to_all x1, starting transfers between devices, local(): lax.all_to_all(pulses[0, 0].transpose(1, 0, 2), 'tile', split_axis=0, con...  11.3 us
    ppermute x2, waiting for transfers between devices, ring_of_lines(): below = lax.ppermute(line, 'tile', up)  10 us
    unnamed x10, local copies, waits for them, and re-layouts  9.68 us
    pallas_call x1, Pallas kernels, parent_sums(): pl.pallas_call(lambda *refs: image_kernel(*refs, steps=steps), out_shape=...  9.45 us
  transfers between devices with their start and end apart: 24, of which 7 were waited for; matrix products, arithmetic and copies ran while one was open for 7% of the time, Pallas kernels for 16%

profile of v2, /device:TPU:1, one launch (start us, length us, event | category | flops | bytes accessed | tf_op | source)
XLA Modules:
  0.0 204.7 jit_solution(14376593452622726730)
XLA Ops:
  2.1 3.4 %copy-done = bf16[4096,1024]{1,0:T(8,128)(2,1)S(1)} copy-done((bf16[4096,1024]{1,0:T(8,128)(2,1)S(1)}, bf16[4096,1024]{1,0:T(8,128)(2,1)}, u32[]{:S(2)}) %copy-start) | copy-done | bytes 8388632
  5.5 11.5 %frame.1.refs_7_.refs_5_ = bf16[4352,1024]{1,0:T(8,128)(2,1)} custom-call(s32[1]{0:T(128)S(6)} %sub.21.info, s32[2,1024]{1,0:T(2,128)S(1)} %pad_add_fusion.band_ref, bf16[4096,1024]{1,0:T(8,128)(2,1)S(1)} %copy-done, bf16[4096,1024]{1,0:T(8,128)(2,1)S(1)} %copy-done), custom_call_target="tpu_custom_call" | custom-call | flops 4563402752 | bytes 26738688 | tf_op jit(solution)/shard_map/frame/pallas_call | solution.py:91
  17.0 1.4 collective-permute-start.15
  18.4 3.5 %copy.24 = bf16[1,1,2,64,8192]{4,2,3,1,0:T(2,128)(2,1)} copy(bf16[1,1,2,64,8192]{4,3,2,1,0:T(8,128)(2,1)S(1)} %copy-done.1) | data formatting | bytes 4194304 | tf_op args[0]
  21.9 11.3 %all-to-all-start = ((bf16[64,2,8192]{2,1,0:T(2,128)(2,1)}), bf16[64,2,8192]{2,1,0:T(2,128)(2,1)S(1)}, u32[]{:S(2)}, u32[]{:S(2)}) async-start(bf16[64,2,8192]{2,1,0:T(2,128)(2,1)} %bitcast.94), calls=%async_computation | async-start | bytes 4194304 | tf_op jit(solution)/shard_map/all_to_all | solution.py:362
  33.3 30.4 %all-to-all-done = bf16[64,2,8192]{2,1,0:T(2,128)(2,1)S(1)} async-done(((bf16[64,2,8192]{2,1,0:T(2,128)(2,1)}), bf16[64,2,8192]{2,1,0:T(2,128)(2,1)S(1)}, u32[]{:S(2)}, u32[]{:S(2)}) %all-to-all-start) | async-done | bytes 2097184 | tf_op jit(solution)/shard_map/all_to_all | solution.py:362
  65.8 2.3 %collective-permute-start.3 = (bf16[16,8192]{1,0:T(8,128)(2,1)S(1)}, bf16[16,8192]{1,0:T(8,128)(2,1)S(1)}, u32[]{:S(2)}, u32[]{:S(2)}) collective-permute-start(bf16[16,8192]{1,0:T(8,128)(2,1)S(1)} %bitcast.106), channel_id=1, source_target_pairs={{0,96},{2,98},{4,100},{6,102},{8,104},{10,106},{12,108},{14,110},{... | collective-permute-start | bytes 786440 | tf_op jit(solution)/shard_map/ppermute | solution.py:39
  68.1 6.5 %collective-permute-done.8 = bf16[16,8192]{1,0:T(8,128)(2,1)S(1)} collective-permute-done((bf16[16,8192]{1,0:T(8,128)(2,1)S(1)}, bf16[16,8192]{1,0:T(8,128)(2,1)S(1)}, u32[]{:S(2)}, u32[]{:S(2)}) %collective-permute-start.8) | collective-permute-done | bytes 262176 | tf_op jit(solution)/shard_map/ppermute | solution.py:56
  74.6 2.7 %collective-permute-start.10 = (bf16[16,8192]{1,0:T(8,128)(2,1)S(1)}, bf16[16,8192]{1,0:T(8,128)(2,1)S(1)}, u32[]{:S(2)}, u32[]{:S(2)}) collective-permute-start(bf16[16,8192]{1,0:T(8,128)(2,1)S(1)} %collective-permute-done.8), channel_id=1, source_target_pairs={{0,12},{2,14},{4,0},{6,2},{8,4},{10,6},{12,8},{14,10},{16,28},{18,... | collective-permute-start | bytes 786440 | tf_op jit(solution)/shard_map/ppermute | solution.py:39
  77.8 2.4 %collective-permute-start.5 = (bf16[16,4096]{1,0:T(8,128)(2,1)S(1)}, bf16[16,4096]{1,0:T(8,128)(2,1)S(1)}, u32[]{:S(2)}, u32[]{:S(2)}) collective-permute-start(bf16[16,4096]{1,0:T(8,128)(2,1)S(1)} %slice.43), channel_id=1, source_target_pairs={{0,96},{2,98},{4,100},{6,102},{8,104},{10,106},{12,108},{14,110},{... | collective-permute-start | bytes 393224 | tf_op jit(solution)/shard_map/ppermute | solution.py:41
  80.2 2.5 %collective-permute-done.9 = bf16[16,8192]{1,0:T(8,128)(2,1)S(1)} collective-permute-done((bf16[16,8192]{1,0:T(8,128)(2,1)S(1)}, bf16[16,8192]{1,0:T(8,128)(2,1)S(1)}, u32[]{:S(2)}, u32[]{:S(2)}) %collective-permute-start.9) | collective-permute-done | bytes 262176 | tf_op jit(solution)/shard_map/ppermute | solution.py:38
  82.7 1.9 collective-permute-start
  84.7 2.7 %collective-permute-start.12 = (bf16[16,4096]{1,0:T(8,128)(2,1)S(1)}, bf16[16,4096]{1,0:T(8,128)(2,1)S(1)}, u32[]{:S(2)}, u32[]{:S(2)}) collective-permute-start(bf16[16,4096]{1,0:T(8,128)(2,1)S(1)} %slice.45), channel_id=1, source_target_pairs={{0,12},{2,14},{4,0},{6,2},{8,4},{10,6},{12,8},{14,10},{16,28},{18,... | collective-permute-start | bytes 393224 | tf_op jit(solution)/shard_map/ppermute | solution.py:41
  87.6 3.4 %collective-permute-done.11 = bf16[16,4096]{1,0:T(8,128)(2,1)S(1)} collective-permute-done((bf16[16,4096]{1,0:T(8,128)(2,1)S(1)}, bf16[16,4096]{1,0:T(8,128)(2,1)S(1)}, u32[]{:S(2)}, u32[]{:S(2)}) %collective-permute-start.11) | collective-permute-done | bytes 131104 | tf_op jit(solution)/shard_map/ppermute | solution.py:40
  92.4 2.3 %collective-permute-start.14 = (bf16[64,8192]{1,0:T(8,128)(2,1)}, bf16[64,8192]{1,0:T(8,128)(2,1)}, u32[]{:S(2)}, u32[]{:S(2)}) collective-permute-start(bf16[64,8192]{1,0:T(8,128)(2,1)} %maximum_maximum_fusion.1.refs_4_), channel_id=1, source_target_pairs={{0,96},{2,98},{4,100},{6,102},{8,104},{10,106},{12,108},{14,110},{... | collective-permute-start | bytes 3145736 | tf_op jit(solution)/shard_map/ppermute | solution.py:48
  94.7 2.8 %copy.25 = f32[1,8,64,1024]{3,1,2,0:T(8,128)S(1)} copy(f32[1,8,64,1024]{3,2,1,0:T(8,128)} %param.14) | data formatting | bytes 4194304 | tf_op args[6]
  97.7 5.3 %phases.1.refs_2_ = bf16[1024,1024]{1,0:T(8,128)(2,1)} custom-call(s32[64]{0:T(128)S(1)} %stack.284.refs_0_, f32[64,8,1024]{2,1,0:T(8,128)S(1)} %bitcast.101), custom_call_target="tpu_custom_call" | custom-call | flops 20971520 | bytes 4194304 | tf_op jit(solution)/shard_map/phases/pallas_call | solution.py:140
  103.0 10.0 %collective-permute-done.6.refs_2_ = bf16[64,8192]{1,0:T(8,128)(2,1)} collective-permute-done((bf16[64,8192]{1,0:T(8,128)(2,1)S(1)}, bf16[64,8192]{1,0:T(8,128)(2,1)}, u32[]{:S(2)}, u32[]{:S(2)}) %collective-permute-start.6) | collective-permute-done | bytes 1048608 | tf_op jit(solution)/shard_map/ppermute | solution.py:47
  113.0 1.4 collective-permute-start.1
  115.8 1.1 slice.46
  116.9 1.1 slice.47
  118.0 2.7 %collective-permute-start.17 = (bf16[32,8192]{1,0:T(8,128)(2,1)S(1)}, bf16[32,8192]{1,0:T(8,128)(2,1)S(1)}, u32[]{:S(2)}, u32[]{:S(2)}) collective-permute-start(bf16[32,8192]{1,0:T(8,128)(2,1)S(1)} %slice.47), channel_id=1, source_target_pairs={{0,12},{2,14},{4,0},{6,2},{8,4},{10,6},{12,8},{14,10},{16,28},{18,... | collective-permute-start | bytes 1572872 | tf_op jit(solution)/shard_map/ppermute | solution.py:50
  120.8 1.1 slice.48
  122.3 1.1 slice.49
  123.4 2.4 %collective-permute-start.19 = (bf16[32,8192]{1,0:T(8,128)(2,1)S(1)}, bf16[32,8192]{1,0:T(8,128)(2,1)S(1)}, u32[]{:S(2)}, u32[]{:S(2)}) collective-permute-start(bf16[32,8192]{1,0:T(8,128)(2,1)S(1)} %slice.49), channel_id=1, source_target_pairs={{0,96},{2,98},{4,100},{6,102},{8,104},{10,106},{12,108},{14,110},{... | collective-permute-start | bytes 1572872 | tf_op jit(solution)/shard_map/ppermute | solution.py:50
  125.7 16.4 %interp.2 = (bf16[2,192,1024]{2,1,0:T(8,128)(2,1)S(1)}, bf16[2,192,1024]{2,1,0:T(8,128)(2,1)S(1)}) custom-call(s32[3]{0:T(128)S(1)} %pad_add_fusion.3.refs_0_, bf16[64,8192]{1,0:T(8,128)(2,1)S(1)} %maximum_maximum_fusion.refs_1_, bf16[64,8192]{1,0:T(8,128)(2,1)} %collective-permute-done.6.refs_2_, bf16[64,8192]{1,0:T(8,128)(2,1)} %collective-permute-done.7.refs_3_, ...), custom_call_target="tpu_custom_call" | custom-call | flops 6845104128 | bytes 24117248 | tf_op jit(solution)/shard_map/interp/pallas_call | solution.py:227
  142.2 1.8 collective-permute-start.20
  143.9 11.0 %interp.3 = (bf16[2,64,1024]{2,1,0:T(8,128)(2,1)S(1)}, bf16[2,64,1024]{2,1,0:T(8,128)(2,1)S(1)}) custom-call(s32[3]{0:T(128)S(1)} %pad_add_fusion.3.refs_0_, bf16[32,8192]{1,0:T(8,128)(2,1)S(1)} %collective-permute-done.16.refs_1_, bf16[32,8192]{1,0:T(8,128)(2,1)S(1)} %collective-permute-done.17.refs_2_, ...), custom_call_target="tpu_custom_call" | custom-call | flops 2281701376 | bytes 19922944 | tf_op jit(solution)/shard_map/interp/pallas_call | solution.py:227
  155.2 1.5 collective-permute-done.21.refs_7_
  156.6 9.5 %image.1 = bf16[2048,512]{1,0:T(8,128)(2,1)S(1)} custom-call(s32[3]{0:T(128)S(1)} %pad_add_fusion.3.refs_0_, s32[2,64]{1,0:T(2,128)S(1)} %pad_add_fusion.1.refs_1_, bf16[1024,1024]{1,0:T(8,128)(2,1)} %phases.1.refs_2_, bf16[1024,1024]{1,0:T(8,128)(2,1)S(1)} %collective-permute-done.1.refs_3_, bf16[2,192,1024]{2,1,0:T(8,128)(2,1)S(1)} %get-tuple-element.9.refs_4_, ...), custom_call_target="tpu_custom_call" | custom-call | flops 4294967296 | bytes 8388608 | tf_op jit(solution)/shard_map/image/pallas_call | solution.py:322
  166.1 34.1 %all_to_all.14 = bf16[128,16,512]{2,1,0:T(8,128)(2,1)S(1)} all-to-all(bf16[128,16,512]{2,1,0:T(8,128)(2,1)S(1)} %bitcast.102), channel_id=1, replica_groups=mesh['tile'=64,'sub'=2] {'tile','sub'}, dimensions={0} | all-to-all | bytes 4194304 | tf_op jit(solution)/shard_map/all_to_all | solution.py:390
  200.9 3.1 %collective-permute-done.22 = f32[16,1024]{1,0:T(8,128)S(1)} collective-permute-done((f32[16,1024]{1,0:T(8,128)S(1)}, f32[16,1024]{1,0:T(8,128)S(1)}, u32[]{:S(2)}, u32[]{:S(2)}) %collective-permute-start.22) | collective-permute-done | bytes 65568 | tf_op jit(solution)/shard_map/ppermute | solution.py:394
  (61 shorter events, 9.4 us)
Async XLA Ops:
  2.1 3.4 %copy-start = (bf16[4096,1024]{1,0:T(8,128)(2,1)S(1)}, bf16[4096,1024]{1,0:T(8,128)(2,1)}, u32[]{:S(2)}) copy-start(bf16[4096,1024]{1,0:T(8,128)(2,1)} %now_ref.1) | copy-start | bytes 25165828
  5.5 12.9 %copy-start.1 = (bf16[1,1,2,64,8192]{4,3,2,1,0:T(8,128)(2,1)S(1)}, bf16[1,1,2,64,8192]{4,3,2,1,0:T(8,128)(2,1)}, u32[]{:S(2)}) copy-start(bf16[1,1,2,64,8192]{4,3,2,1,0:T(8,128)(2,1)} %param.8) | copy-start | bytes 6291460
  17.0 106.4 %collective-permute-start.15 = (bf16[4352,1024]{1,0:T(8,128)(2,1)}, bf16[4352,1024]{1,0:T(8,128)(2,1)}, u32[]{:S(2)}, u32[]{:S(2)}) collective-permute-start(bf16[4352,1024]{1,0:T(8,128)(2,1)} %frame.1.refs_7_.refs_5_), channel_id=1, source_target_pairs={{0,2},{2,0},{4,6},{6,4},{8,10},{10,8},{12,14},{14,12},{16,18},{18,... | collective-permute-start | bytes 26738696 | tf_op jit(solution)/shard_map/ppermute | solution.py:378
  21.9 11.3 %copy-start.3 = (s32[8]{0:T(128)S(1)}, s32[8]{0:T(128)}, u32[]{:S(2)}) copy-start(s32[8]{0:T(128)} %param.13) | copy-start | bytes 100
  21.9 41.9 %all-to-all-start = ((bf16[64,2,8192]{2,1,0:T(2,128)(2,1)}), bf16[64,2,8192]{2,1,0:T(2,128)(2,1)S(1)}, u32[]{:S(2)}, u32[]{:S(2)}) async-start(bf16[64,2,8192]{2,1,0:T(2,128)(2,1)} %bitcast.94), calls=%async_computation | async-start | bytes 4194304 | tf_op jit(solution)/shard_map/all_to_all | solution.py:362
  33.2 46.9 %copy-start.2 = (s32[64,1]{0,1:T(1,128)S(1)}, s32[64,1]{0,1:T(1,128)}, u32[]{:S(2)}) copy-start(s32[64,1]{0,1:T(1,128)} %param.15) | copy-start | bytes 772
  65.3 9.3 %collective-permute-start.8 = (bf16[16,8192]{1,0:T(8,128)(2,1)S(1)}, bf16[16,8192]{1,0:T(8,128)(2,1)S(1)}, u32[]{:S(2)}, u32[]{:S(2)}) collective-permute-start(bf16[16,8192]{1,0:T(8,128)(2,1)S(1)} %bitcast.104), channel_id=1, source_target_pairs={{0,16},{2,18},{4,20},{6,22},{8,24},{10,26},{12,28},{14,30},{16,0},... | collective-permute-start | bytes 786440 | tf_op jit(solution)/shard_map/ppermute | solution.py:56
  65.4 11.9 %collective-permute-start.2 = (bf16[16,8192]{1,0:T(8,128)(2,1)S(1)}, bf16[16,8192]{1,0:T(8,128)(2,1)S(1)}, u32[]{:S(2)}, u32[]{:S(2)}) collective-permute-start(bf16[16,8192]{1,0:T(8,128)(2,1)S(1)} %bitcast.105), channel_id=1, source_target_pairs={{0,32},{2,34},{4,36},{6,38},{8,40},{10,42},{12,44},{14,46},{16,48}... | collective-permute-start | bytes 786440 | tf_op jit(solution)/shard_map/ppermute | solution.py:38
  65.8 11.9 %collective-permute-start.3 = (bf16[16,8192]{1,0:T(8,128)(2,1)S(1)}, bf16[16,8192]{1,0:T(8,128)(2,1)S(1)}, u32[]{:S(2)}, u32[]{:S(2)}) collective-permute-start(bf16[16,8192]{1,0:T(8,128)(2,1)S(1)} %bitcast.106), channel_id=1, source_target_pairs={{0,96},{2,98},{4,100},{6,102},{8,104},{10,106},{12,108},{14,110},{... | collective-permute-start | bytes 786440 | tf_op jit(solution)/shard_map/ppermute | solution.py:39
  74.6 8.1 %collective-permute-start.9 = (bf16[16,8192]{1,0:T(8,128)(2,1)S(1)}, bf16[16,8192]{1,0:T(8,128)(2,1)S(1)}, u32[]{:S(2)}, u32[]{:S(2)}) collective-permute-start(bf16[16,8192]{1,0:T(8,128)(2,1)S(1)} %collective-permute-done.8), channel_id=1, source_target_pairs={{0,4},{2,6},{4,8},{6,10},{8,12},{10,14},{12,0},{14,2},{16,20},{18,... | collective-permute-start | bytes 786440 | tf_op jit(solution)/shard_map/ppermute | solution.py:38
  74.6 9.9 %collective-permute-start.10 = (bf16[16,8192]{1,0:T(8,128)(2,1)S(1)}, bf16[16,8192]{1,0:T(8,128)(2,1)S(1)}, u32[]{:S(2)}, u32[]{:S(2)}) collective-permute-start(bf16[16,8192]{1,0:T(8,128)(2,1)S(1)} %collective-permute-done.8), channel_id=1, source_target_pairs={{0,12},{2,14},{4,0},{6,2},{8,4},{10,6},{12,8},{14,10},{16,28},{18,... | collective-permute-start | bytes 786440 | tf_op jit(solution)/shard_map/ppermute | solution.py:39
  77.3 7.4 %collective-permute-start.4 = (bf16[16,4096]{1,0:T(8,128)(2,1)S(1)}, bf16[16,4096]{1,0:T(8,128)(2,1)S(1)}, u32[]{:S(2)}, u32[]{:S(2)}) collective-permute-start(bf16[16,4096]{1,0:T(8,128)(2,1)S(1)} %slice.42), channel_id=1, source_target_pairs={{0,32},{2,34},{4,36},{6,38},{8,40},{10,42},{12,44},{14,46},{16,48}... | collective-permute-start | bytes 393224 | tf_op jit(solution)/shard_map/ppermute | solution.py:40
  77.8 9.6 %collective-permute-start.5 = (bf16[16,4096]{1,0:T(8,128)(2,1)S(1)}, bf16[16,4096]{1,0:T(8,128)(2,1)S(1)}, u32[]{:S(2)}, u32[]{:S(2)}) collective-permute-start(bf16[16,4096]{1,0:T(8,128)(2,1)S(1)} %slice.43), channel_id=1, source_target_pairs={{0,96},{2,98},{4,100},{6,102},{8,104},{10,106},{12,108},{14,110},{... | collective-permute-start | bytes 393224 | tf_op jit(solution)/shard_map/ppermute | solution.py:41
  82.7 9.8 %collective-permute-start = (s32[65]{0:T(128)S(1)}, s32[65]{0:T(128)S(1)}, u32[]{:S(2)}, u32[]{:S(2)}) collective-permute-start(s32[65]{0:T(128)S(1)} %pad_add_fusion.2), channel_id=1, source_target_pairs={{0,2},{2,0},{4,6},{6,4},{8,10},{10,8},{12,14},{14,12},{16,18},{18,... | collective-permute-start | bytes 788 | tf_op jit(solution)/shard_map/ppermute | solution.py:377
  84.6 6.4 %collective-permute-start.11 = (bf16[16,4096]{1,0:T(8,128)(2,1)S(1)}, bf16[16,4096]{1,0:T(8,128)(2,1)S(1)}, u32[]{:S(2)}, u32[]{:S(2)}) collective-permute-start(bf16[16,4096]{1,0:T(8,128)(2,1)S(1)} %slice.44), channel_id=1, source_target_pairs={{0,4},{2,6},{4,8},{6,10},{8,12},{10,14},{12,0},{14,2},{16,20},{18,... | collective-permute-start | bytes 393224 | tf_op jit(solution)/shard_map/ppermute | solution.py:40
  84.7 6.3 %collective-permute-start.12 = (bf16[16,4096]{1,0:T(8,128)(2,1)S(1)}, bf16[16,4096]{1,0:T(8,128)(2,1)S(1)}, u32[]{:S(2)}, u32[]{:S(2)}) collective-permute-start(bf16[16,4096]{1,0:T(8,128)(2,1)S(1)} %slice.45), channel_id=1, source_target_pairs={{0,12},{2,14},{4,0},{6,2},{8,4},{10,6},{12,8},{14,10},{16,28},{18,... | collective-permute-start | bytes 393224 | tf_op jit(solution)/shard_map/ppermute | solution.py:41
  87.5 25.5 %collective-permute-start.6 = (bf16[64,8192]{1,0:T(8,128)(2,1)S(1)}, bf16[64,8192]{1,0:T(8,128)(2,1)}, u32[]{:S(2)}, u32[]{:S(2)}) collective-permute-start(bf16[64,8192]{1,0:T(8,128)(2,1)S(1)} %maximum_maximum_fusion.refs_1_), channel_id=1, source_target_pairs={{0,4},{2,6},{4,8},{6,10},{8,12},{10,14},{12,0},{14,2},{16,20},{18,... | collective-permute-start | bytes 3145736 | tf_op jit(solution)/shard_map/ppermute | solution.py:47
  91.0 25.9 %collective-permute-start.7 = (bf16[64,8192]{1,0:T(8,128)(2,1)S(1)}, bf16[64,8192]{1,0:T(8,128)(2,1)}, u32[]{:S(2)}, u32[]{:S(2)}) collective-permute-start(bf16[64,8192]{1,0:T(8,128)(2,1)S(1)} %maximum_maximum_fusion.refs_1_), channel_id=1, source_target_pairs={{0,12},{2,14},{4,0},{6,2},{8,4},{10,6},{12,8},{14,10},{16,28},{18,... | collective-permute-start | bytes 3145736 | tf_op jit(solution)/shard_map/ppermute | solution.py:48
  92.0 26.0 %collective-permute-start.13 = (bf16[64,8192]{1,0:T(8,128)(2,1)}, bf16[64,8192]{1,0:T(8,128)(2,1)}, u32[]{:S(2)}, u32[]{:S(2)}) collective-permute-start(bf16[64,8192]{1,0:T(8,128)(2,1)} %maximum_maximum_fusion.1.refs_4_), channel_id=1, source_target_pairs={{0,32},{2,34},{4,36},{6,38},{8,40},{10,42},{12,44},{14,46},{16,48}... | collective-permute-start | bytes 3145736 | tf_op jit(solution)/shard_map/ppermute | solution.py:47
  92.4 29.4 %collective-permute-start.14 = (bf16[64,8192]{1,0:T(8,128)(2,1)}, bf16[64,8192]{1,0:T(8,128)(2,1)}, u32[]{:S(2)}, u32[]{:S(2)}) collective-permute-start(bf16[64,8192]{1,0:T(8,128)(2,1)} %maximum_maximum_fusion.1.refs_4_), channel_id=1, source_target_pairs={{0,96},{2,98},{4,100},{6,102},{8,104},{10,106},{12,108},{14,110},{... | collective-permute-start | bytes 3145736 | tf_op jit(solution)/shard_map/ppermute | solution.py:48
  113.0 42.1 %collective-permute-start.1 = (bf16[1024,1024]{1,0:T(8,128)(2,1)}, bf16[1024,1024]{1,0:T(8,128)(2,1)S(1)}, u32[]{:S(2)}, u32[]{:S(2)}) collective-permute-start(bf16[1024,1024]{1,0:T(8,128)(2,1)} %phases.1.refs_2_), channel_id=1, source_target_pairs={{0,2},{2,0},{4,6},{6,4},{8,10},{10,8},{12,14},{14,12},{16,18},{18,... | collective-permute-start | bytes 6291464 | tf_op jit(solution)/shard_map/ppermute | solution.py:379
  116.8 25.3 %collective-permute-start.16 = (bf16[32,8192]{1,0:T(8,128)(2,1)S(1)}, bf16[32,8192]{1,0:T(8,128)(2,1)S(1)}, u32[]{:S(2)}, u32[]{:S(2)}) collective-permute-start(bf16[32,8192]{1,0:T(8,128)(2,1)S(1)} %slice.46), channel_id=1, source_target_pairs={{0,4},{2,6},{4,8},{6,10},{8,12},{10,14},{12,0},{14,2},{16,20},{18,... | collective-permute-start | bytes 1572872 | tf_op jit(solution)/shard_map/ppermute | solution.py:49
  118.0 25.9 %collective-permute-start.17 = (bf16[32,8192]{1,0:T(8,128)(2,1)S(1)}, bf16[32,8192]{1,0:T(8,128)(2,1)S(1)}, u32[]{:S(2)}, u32[]{:S(2)}) collective-permute-start(bf16[32,8192]{1,0:T(8,128)(2,1)S(1)} %slice.47), channel_id=1, source_target_pairs={{0,12},{2,14},{4,0},{6,2},{8,4},{10,6},{12,8},{14,10},{16,28},{18,... | collective-permute-start | bytes 1572872 | tf_op jit(solution)/shard_map/ppermute | solution.py:50
  121.8 22.1 %collective-permute-start.18 = (bf16[32,8192]{1,0:T(8,128)(2,1)S(1)}, bf16[32,8192]{1,0:T(8,128)(2,1)S(1)}, u32[]{:S(2)}, u32[]{:S(2)}) collective-permute-start(bf16[32,8192]{1,0:T(8,128)(2,1)S(1)} %slice.48), channel_id=1, source_target_pairs={{0,32},{2,34},{4,36},{6,38},{8,40},{10,42},{12,44},{14,46},{16,48}... | collective-permute-start | bytes 1572872 | tf_op jit(solution)/shard_map/ppermute | solution.py:49
  123.4 20.6 %collective-permute-start.19 = (bf16[32,8192]{1,0:T(8,128)(2,1)S(1)}, bf16[32,8192]{1,0:T(8,128)(2,1)S(1)}, u32[]{:S(2)}, u32[]{:S(2)}) collective-permute-start(bf16[32,8192]{1,0:T(8,128)(2,1)S(1)} %slice.49), channel_id=1, source_target_pairs={{0,96},{2,98},{4,100},{6,102},{8,104},{10,106},{12,108},{14,110},{... | collective-permute-start | bytes 1572872 | tf_op jit(solution)/shard_map/ppermute | solution.py:50
  142.2 14.5 %collective-permute-start.20 = (bf16[2,192,1024]{2,1,0:T(8,128)(2,1)S(1)}, bf16[2,192,1024]{2,1,0:T(8,128)(2,1)S(1)}, u32[]{:S(2)}, u32[]{:S(2)}) collective-permute-start(bf16[2,192,1024]{2,1,0:T(8,128)(2,1)S(1)} %get-tuple-element.11), channel_id=1, source_target_pairs={{0,2},{2,0},{4,6},{6,4},{8,10},{10,8},{12,14},{14,12},{16,18},{18,... | collective-permute-start | bytes 2359304 | tf_op jit(solution)/shard_map/ppermute | solution.py:387
  155.0 1.6 collective-permute-start.21
  200.5 3.6 %collective-permute-start.22 = (f32[16,1024]{1,0:T(8,128)S(1)}, f32[16,1024]{1,0:T(8,128)S(1)}, u32[]{:S(2)}, u32[]{:S(2)}) collective-permute-start(f32[16,1024]{1,0:T(8,128)S(1)} %bitcast.108), channel_id=1, source_target_pairs={{0,1},{1,0},{2,3},{3,2},{4,5},{5,4},{6,7},{7,6},{8,9},{9,8},{10,11... | collective-permute-start | bytes 196616 | tf_op jit(solution)/shard_map/ppermute | solution.py:394
